TPU v7x, 128 devices: a whole 4x4x4 slice. The times are simulated.
128 devices in a mesh: row: 8 (over y, x_lo), col: 16 (over z, x_hi, core).
Axes of the slice: x: 4 (x_hi: 2, x_lo: 2; x = x_hi * 2 + x_lo), y: 4, z: 4, core: 2. Of those that a mesh axis runs over, the one named last changes fastest.
Arguments:
- tokens: bfloat16 [16384, 3584], P(('row', 'col')), may hold values from -6 to 6
- expert_ids: int32 [16384, 4], P(('row', 'col')), may hold values from 0 to 127, all different within a row; in each aligned block of 128 rows (0 to 127, 128 to 255, ...) at most 5 rows name the same one
- combine_weights: float32 [16384, 4], P(('row', 'col')), may hold values from 0.1 to 1
- expert_gate: bfloat16 [128, 3584, 1024], P(('row', 'col')), may hold values from -0.09375 to 0.09375
- expert_up: bfloat16 [128, 3584, 1024], P(('row', 'col')), may hold values from -0.09375 to 0.09375
- expert_down: bfloat16 [128, 1024, 3584], P(('row', 'col')), may hold values from -0.1875 to 0.1875
- shared_gate: bfloat16 [3584, 1024], P(None, 'row'), may hold values from -0.09375 to 0.09375
- shared_up: bfloat16 [3584, 1024], P(None, 'row'), may hold values from -0.09375 to 0.09375
- shared_down: bfloat16 [1024, 3584], P('row'), may hold values from -0.1875 to 0.1875
Outputs:
- mixed: bfloat16 [16384, 3584], P(('row', 'col'))
Inputs may be any that keep to these rules, and one draw needn't show every extreme that they name: `expert_ids`: each row names 4 different experts. Among the 128 rows of one device no expert is named by more than 5 rows, and in every draw some expert is named by exactly 5 rows of some device.
All inputs are finite; a program needn't handle non-finite values.
Results may differ from a plain program's by a relative error of at most 0.0055.
Values may be sent and summed in bfloat16 or wider, within the bound.
A program may use at most 128 MiB of HBM per device.

v0:
```python
import jax
import jax.numpy as jnp
from jax import lax
from jax.sharding import Mesh
from jax.sharding import PartitionSpec as P

ROW = ("row_0", "row_1")
ROW_COL = ("row_0", "row_1", "col")


def own_rows(running, axes):
    for axis in axes:
        running = lax.psum_scatter(running, axis, scatter_dimension=0, tiled=True)
    return running


def expert_mlp(token_rows, gate_w, up_w, down_w):
    gate_proj = jnp.dot(token_rows, gate_w, preferred_element_type=jnp.float32)
    up_proj = jnp.dot(token_rows, up_w, preferred_element_type=jnp.float32)
    hidden = (jax.nn.silu(gate_proj) * up_proj).astype(jnp.bfloat16)
    return jnp.dot(hidden, down_w, preferred_element_type=jnp.float32).astype(jnp.bfloat16)


def place_slots(choices, experts, capacity):
    flat_ids = choices.reshape(-1)
    onehot = (flat_ids[:, None] == jnp.arange(experts, dtype=jnp.int32)[None, :]).astype(jnp.int32)
    running = jnp.cumsum(onehot, axis=0)
    slot_rank = jnp.sum(onehot * running, axis=1) - 1
    return flat_ids * capacity + slot_rank


def per_device(
    tokens,
    expert_ids,
    combine_weights,
    expert_gate,
    expert_up,
    expert_down,
    shared_gate,
    shared_up,
    shared_down,
):
    rows_here, model_width = tokens.shape
    choices_each = expert_ids.shape[1]
    row_devices = lax.axis_size(ROW)
    col_devices = lax.axis_size("col")
    experts = row_devices * col_devices
    capacity = max(2, 5 * rows_here * choices_each // (4 * experts))
    target = place_slots(expert_ids, experts, capacity)
    owner_row = jnp.arange(rows_here * choices_each, dtype=jnp.int32) // choices_each
    source_table = jnp.full((experts * capacity,), -1, jnp.int32).at[target].set(owner_row)
    filled = source_table >= 0
    outgoing = jnp.where(
        filled[:, None], tokens[jnp.maximum(source_table, 0)], jnp.zeros((), jnp.bfloat16)
    )
    arrived = lax.all_to_all(
        outgoing.reshape(experts, capacity, model_width),
        ROW_COL,
        split_axis=0,
        concat_axis=0,
        tiled=True,
    )
    results = expert_mlp(
        arrived.reshape(-1, model_width), expert_gate[0], expert_up[0], expert_down[0]
    )
    returned = lax.all_to_all(
        results.reshape(experts, capacity, model_width),
        ROW_COL,
        split_axis=0,
        concat_axis=0,
        tiled=True,
    )
    returned = returned.reshape(-1, model_width)
    picked = returned[target].reshape(rows_here, choices_each, model_width)
    routed = jnp.sum(picked.astype(jnp.float32) * combine_weights[:, :, None], axis=1)
    shard_rows = lax.all_gather(tokens, ROW, axis=0, tiled=True)
    gate_proj = jnp.dot(shard_rows, shared_gate, preferred_element_type=jnp.float32)
    up_proj = jnp.dot(shard_rows, shared_up, preferred_element_type=jnp.float32)
    shared_hidden = (jax.nn.silu(gate_proj) * up_proj).astype(jnp.bfloat16)
    shared = own_rows(jnp.dot(shared_hidden, shared_down, preferred_element_type=jnp.float32), ROW)
    return (routed + shared).astype(jnp.bfloat16)


def solution(mesh):
    finer = Mesh(mesh.devices.reshape(4, 2, mesh.shape["col"]), ("row_0", "row_1", "col"))
    placed = (
        P(ROW_COL, None),
        P(ROW_COL, None),
        P(ROW_COL, None),
        P(ROW_COL, None, None),
        P(ROW_COL, None, None),
        P(ROW_COL, None, None),
        P(None, ROW),
        P(None, ROW),
        P(ROW, None),
    )
    return jax.shard_map(
        per_device, mesh=finer, in_specs=placed, out_specs=P(ROW_COL, None), check_vma=False
    )
```

profile of v0, /device:TPU:32, one launch (start us, length us, event | category | flops | bytes accessed | tf_op | source)
XLA Modules:
  0.0 588.3 jit_solution(16821377509099226746)
XLA Ops:
  6.5 0.7 all-gather.2.cloned.1.call-update
  7.3 152.4 %all-gather.2.cloned.1.call-done = bf16[1024,3584]{1,0:T(8,128)(2,1)} async-done(((bf16[128,3584]{1,0:T(8,128)(2,1)}), bf16[1024,3584]{1,0:T(8,128)(2,1)}) %all-gather.2.cloned.1.call-update) | async-done | bytes 7340048 | tf_op jit(solution)/shard_map/all_gather | solution.py:76
  159.7 5.3 fusion.33
  165.1 15.9 %fusion.15 = f32[1024,3584]{1,0:T(8,128)} fusion(bf16[128,3584]{1,0:T(8,128)(2,1)S(1)} %copy-done, bf16[1024,3584]{1,0:T(8,128)(2,1)} %all-gather.2.cloned.1.call-done, bf16[3584,128]{1,0:T(8,128)(2,1)S(1)} %copy-done.3, f32[1024,128]{1,0:T(8,128)S(1)} %fusion.33), kind=kOutput, calls=%fused_computation.17 | convolution fusion | flops 1879834624 | bytes 24379392 | tf_op jit(solution)/shard_map/dot_general | solution.py:80
  181.1 0.6 copy-done.4
  182.7 0.2 fusion.21
  182.9 2.4 scatter_custom_fusion
  185.4 0.2 broadcast_in_dim.26
  185.7 5.2 gather_fusion
  190.9 8.1 %gather.9 = bf16[128,5,3584]{2,1,0:T(8,128)(2,1)} reshape(bf16[640,3584]{1,0:T(8,128)(2,1)} %gather_fusion) | data formatting | bytes 9175040 | tf_op jit(solution)/shard_map/gather | solution.py:54
  198.9 4.0 broadcast_select_fusion
  202.9 111.2 %all_to_all.10 = bf16[128,5,3584]{2,1,0:T(8,128)(2,1)} all-to-all(bf16[128,5,3584]{2,1,0:T(8,128)(2,1)S(1)} %broadcast_select_fusion), channel_id=1, replica_groups=mesh['row_0'=4,'row_1'=2,'col'=16] {'row_0','row_1','col'}, dimensions={0} | all-to-all | bytes 9175040 | tf_op jit(solution)/shard_map/all_to_all | solution.py:56
  314.1 8.3 %reshape.73 = bf16[640,3584]{1,0:T(8,128)(2,1)} reshape(bf16[128,5,3584]{2,1,0:T(8,128)(2,1)} %all_to_all.10) | data formatting | bytes 9175040 | tf_op jit(solution)/shard_map/reshape | solution.py:64
  322.4 69.8 %reduce-scatter.3.cloned.1.call-done = f32[256,3584]{1,0:T(8,128)} async-done(((f32[1024,3584]{1,0:T(8,128)}), f32[256,3584]{1,0:T(8,128)}) %reduce-scatter.3.cloned.1.call-update) | async-done | bytes 3670032 | tf_op jit(solution)/shard_map/reduce_scatter | solution.py:13
  392.3 10.9 %fusion.4 = f32[640,1024]{1,0:T(8,128)} fusion(bf16[640,3584]{1,0:T(8,128)(2,1)} %reshape.73, bf16[1,3584,1024]{2,1,0:T(8,128)(2,1)} %param.12), kind=kOutput, calls=%fused_computation.7 | convolution fusion | flops 4697620480 | bytes 14548992 | tf_op jit(solution)/shard_map/dot_general | solution.py:18
  403.2 18.8 %fusion.6 = bf16[640,3584]{1,0:T(8,128)(2,1)} fusion(bf16[1,1024,3584]{2,1,0:T(8,128)(2,1)} %param.14, f32[640,1024]{1,0:T(8,128)} %fusion.4, bf16[640,3584]{1,0:T(8,128)(2,1)} %reshape.73, bf16[1,3584,1024]{2,1,0:T(8,128)(2,1)} %param.13), kind=kOutput, calls=%fused_computation.11 | convolution fusion | flops 9401466880 | bytes 26476544 | tf_op jit(solution)/shard_map/dot_general | solution.py:21
  422.0 7.8 %reshape.74 = bf16[128,5,3584]{2,1,0:T(8,128)(2,1)} reshape(bf16[640,3584]{1,0:T(8,128)(2,1)} %fusion.6) | data formatting | bytes 9175040 | tf_op jit(solution)/shard_map/reshape | solution.py:67
  429.8 11.8 %all-to-all-start.1 = ((bf16[128,5,3584]{2,1,0:T(8,128)(2,1)}), bf16[128,5,3584]{2,1,0:T(8,128)(2,1)}, u32[]{:S(2)}, u32[]{:S(2)}) async-start(bf16[128,5,3584]{2,1,0:T(8,128)(2,1)} %reshape.74), calls=%async_computation.1 | async-start | bytes 14680064 | tf_op jit(solution)/shard_map/all_to_all | solution.py:66
  441.8 102.7 %all-to-all-done.1 = bf16[128,5,3584]{2,1,0:T(8,128)(2,1)} async-done(((bf16[128,5,3584]{2,1,0:T(8,128)(2,1)}), bf16[128,5,3584]{2,1,0:T(8,128)(2,1)}, u32[]{:S(2)}, u32[]{:S(2)}) %all-to-all-start.1) | async-done | bytes 4587552 | tf_op jit(solution)/shard_map/all_to_all | solution.py:66
  544.4 8.1 %reshape.75 = bf16[640,3584]{1,0:T(8,128)(2,1)} reshape(bf16[128,5,3584]{2,1,0:T(8,128)(2,1)} %all-to-all-done.1) | data formatting | bytes 9175040 | tf_op jit(solution)/shard_map/reshape | solution.py:73
  552.6 10.8 %gather_fusion.1 = bf16[512,3584]{1,0:T(8,128)(2,1)} fusion(bf16[640,3584]{1,0:T(8,128)(2,1)} %reshape.75, s32[1024]{0:T(1024)S(1)} %pad_clamp_fusion), kind=kCustom, calls=%fused_computation.1 | custom fusion | bytes 7342080 | tf_op jit(solution)/shard_map/gather | solution.py:74
  563.4 7.5 %reshape.76 = f32[128,4,3584]{2,1,0:T(4,128)} reshape(bf16[512,3584]{1,0:T(8,128)(2,1)} %gather_fusion.1) | data formatting | bytes 11010048 | tf_op jit(solution)/shard_map/convert_element_type | solution.py:75
  570.9 8.3 %multiply_reduce_fusion = f32[128,3584]{1,0:T(8,128)S(1)} fusion(f32[128,4,3584]{2,1,0:T(4,128)} %reshape.76, f32[128,4]{1,0:T(8,128)S(1)} %copy.16), kind=kLoop, calls=%fused_computation.9 | loop fusion | flops 3211264 | bytes 9177088 | tf_op jit(solution)/shard_map/reduce_sum | solution.py:75
  579.2 2.6 add_convert_fusion
  (39 shorter events, 1.3 us)
Async XLA Ops:
  6.5 158.5 %copy-start = (bf16[128,3584]{1,0:T(8,128)(2,1)S(1)}, bf16[128,3584]{1,0:T(8,128)(2,1)}, u32[]{:S(2)}) copy-start(bf16[128,3584]{1,0:T(8,128)(2,1)} %param.17) | copy-start | bytes 2752516
  6.5 153.2 %all-gather.2.cloned.1.call-start = ((), (), s32[]{:S(2)}) async-start(), calls=%async_computation.4 | async-start | bytes 8257536 | tf_op jit(solution)/shard_map/all_gather | solution.py:76
  7.3 157.8 %copy-start.3 = (bf16[3584,128]{1,0:T(8,128)(2,1)S(1)}, bf16[3584,128]{1,0:T(8,128)(2,1)}, u32[]{:S(2)}) copy-start(bf16[3584,128]{1,0:T(8,128)(2,1)} %param.16) | copy-start | bytes 2752516
  7.3 385.0 %reduce-scatter.3.cloned.1.call-start = ((), (), s32[]{:S(2)}) async-start(), calls=%async_computation.5 | async-start | bytes 18350080 | tf_op jit(solution)/shard_map/reduce_scatter | solution.py:13
  181.0 0.7 copy-start.4
  181.0 4.6 copy-start.2
  181.0 398.2 %reduce-scatter.5.cloned.1.call-start = ((), (), s32[]{:S(2)}) async-start(), calls=%async_computation.6 | async-start | bytes 5505024 | tf_op jit(solution)/shard_map/reduce_scatter | solution.py:13
  429.8 11.8 %copy-start.5 = (f32[128,4]{0,1:T(4,128)S(1)}, f32[128,4]{0,1:T(4,128)}, u32[]{:S(2)}) copy-start(f32[128,4]{0,1:T(4,128)} %param.11) | copy-start | bytes 6148
  429.8 114.6 %all-to-all-start.1 = ((bf16[128,5,3584]{2,1,0:T(8,128)(2,1)}), bf16[128,5,3584]{2,1,0:T(8,128)(2,1)}, u32[]{:S(2)}, u32[]{:S(2)}) async-start(bf16[128,5,3584]{2,1,0:T(8,128)(2,1)} %reshape.74), calls=%async_computation.1 | async-start | bytes 14680064 | tf_op jit(solution)/shard_map/all_to_all | solution.py:66
  570.9 10.9 %copy-start.1 = (bf16[128,3584]{1,0:T(8,128)(2,1)S(1)}, bf16[128,3584]{1,0:T(8,128)(2,1)}, u32[]{:S(2)}) copy-start(bf16[128,3584]{1,0:T(8,128)(2,1)} %param.17) | copy-start | bytes 2752516
Sparse Core Ops, SparseCore 0:
  9.0 150.6 all-gather.1
  181.1 211.1 reduce-scatter.2
  394.6 59.4 reduce-scatter.4
where the time goes:
time: 590 us; the launch traced here: 588 us
  waiting for transfers between devices  326 us (55%)
  blocking collectives  111 us (19%)
  local copies, waits for them, and re-layouts  60 us (10%)
  matrix products  50.9 us (9%)
  other arithmetic  15.4 us (3%)
  between operations  13.3 us (2%)
  starting transfers between devices  11.9 us (2%)
    all_gather x1, waiting for transfers between devices, per_device(): shard_rows = lax.all_gather(tokens, ROW, axis=0, tiled=True)  152 us
    all_to_all x1, blocking collectives, per_device(): lax.all_to_all(outgoing.reshape(experts, capacity, model_width), ROW_COL,...  111 us
    all_to_all x1, waiting for transfers between devices, per_device(): lax.all_to_all(results.reshape(experts, capacity, model_width), ROW_COL,...  103 us
    reduce_scatter x2, waiting for transfers between devices, own_rows(): running = lax.psum_scatter(running, axis, scatter_dimension=0, tiled=True)  69.9 us
    dot_general x1, matrix products, expert_mlp(): jnp.dot(hidden, down_w, preferred_element_type=jnp.float32)  18.8 us
    dot_general x1, matrix products, per_device(): jnp.dot(shared_hidden, shared_down, preferred_element_type=jnp.float32)  15.9 us
    gather x2, local copies, waits for them, and re-layouts, per_device(): tokens[jnp.maximum(source_table, 0)]  13.3 us
    all_to_all x1, starting transfers between devices, per_device(): lax.all_to_all(results.reshape(experts, capacity, model_width), ROW_COL,...  11.8 us
  transfers between devices with their start and end apart: 4, of which 3 were waited for; matrix products, arithmetic and copies ran while one was open for 17% of the time, Pallas kernels for 0%

commit v1 on v0

--- a/solution.py
+++ b/solution.py
@@ -73,7 +73,9 @@
     returned = returned.reshape(-1, model_width)
     picked = returned[target].reshape(rows_here, choices_each, model_width)
     routed = jnp.sum(picked.astype(jnp.float32) * combine_weights[:, :, None], axis=1)
-    shard_rows = lax.all_gather(tokens, ROW, axis=0, tiled=True)
+    shard_rows = jnp.concatenate(
+        lax.all_to_all(jnp.stack([tokens] * lax.axis_size(ROW)), ROW, 0, 0), axis=0
+    )
     gate_proj = jnp.dot(shard_rows, shared_gate, preferred_element_type=jnp.float32)
     up_proj = jnp.dot(shard_rows, shared_up, preferred_element_type=jnp.float32)
     shared_hidden = (jax.nn.silu(gate_proj) * up_proj).astype(jnp.bfloat16)

time: 590 us -> 528 us (0.89)
  waiting for transfers between devices: 326 us -> 174 us
  blocking collectives: 111 us -> 200 us
    all_gather x1 -> x0, waiting for transfers between devices: 152 us -> none  [per_device(): shard_rows = lax.all_gather(tokens, ROW, axis=0, tiled=True)]
    all_to_all x0 -> x1, blocking collectives: none -> 89.6 us  [per_device(): lax.all_to_all(jnp.stack([tokens] * lax.axis_size(ROW)), ROW, 0, 0)]
  transfers between devices with their start and end apart: 4 -> 3, of which waited for: 3 -> 2; matrix products, arithmetic and copies ran while one was open for 17% -> 19% of each run, Pallas kernels for 0% -> 0%
where the time goes in v1:
time: 528 us; the launch traced here: 526 us
  blocking collectives  200 us (38%)
  waiting for transfers between devices  174 us (33%)
  local copies, waits for them, and re-layouts  64.6 us (12%)
  matrix products  47.6 us (9%)
  other arithmetic  15.3 us (3%)
  between operations  13.6 us (3%)
  starting transfers between devices  11.8 us (2%)
    all_to_all x1, blocking collectives, per_device(): lax.all_to_all(outgoing.reshape(experts, capacity, model_width), ROW_COL,...  110 us
    all_to_all x1, waiting for transfers between devices, per_device(): lax.all_to_all(results.reshape(experts, capacity, model_width), ROW_COL,...  104 us
    all_to_all x1, blocking collectives, per_device(): lax.all_to_all(jnp.stack([tokens] * lax.axis_size(ROW)), ROW, 0, 0)  89.6 us
    reduce_scatter x2, waiting for transfers between devices, own_rows(): running = lax.psum_scatter(running, axis, scatter_dimension=0, tiled=True)  69.9 us
    dot_general x1, matrix products, expert_mlp(): jnp.dot(hidden, down_w, preferred_element_type=jnp.float32)  18.8 us
    dot_general x1, matrix products, per_device(): jnp.dot(shared_hidden, shared_down, preferred_element_type=jnp.float32)  15.9 us
    gather x2, local copies, waits for them, and re-layouts, per_device(): tokens[jnp.maximum(source_table, 0)]  13.1 us
    all_to_all x1, starting transfers between devices, per_device(): lax.all_to_all(results.reshape(experts, capacity, model_width), ROW_COL,...  11.8 us
  transfers between devices with their start and end apart: 3, of which 2 were waited for; matrix products, arithmetic and copies ran while one was open for 19% of the time, Pallas kernels for 0%

profile of v1, /device:TPU:32, one launch (start us, length us, event | category | flops | bytes accessed | tf_op | source)
XLA Modules:
  0.0 526.4 jit_solution(11594685543665104018)
XLA Ops:
  6.5 1.9 stack.2
  8.4 89.6 %all_to_all.15 = bf16[8,128,3584]{2,1,0:T(8,128)(2,1)S(1)} all-to-all(bf16[8,128,3584]{2,1,0:T(8,128)(2,1)S(1)} %stack.2), channel_id=1, replica_groups=mesh['row_0'=4,'row_1'=2,'col'=16] {'row_0','row_1'}, dimensions={0} | all-to-all | bytes 14680064 | tf_op jit(solution)/shard_map/all_to_all | solution.py:77
  98.1 2.9 copy-done.3
  101.0 2.1 fusion.33
  103.1 15.9 %fusion.15 = f32[1024,3584]{1,0:T(8,128)} fusion(bf16[128,3584]{1,0:T(8,128)(2,1)S(1)} %copy-done, bf16[1024,3584]{1,0:T(8,128)(2,1)} %bitcast.38, bf16[3584,128]{1,0:T(8,128)(2,1)S(1)} %copy-done.4, f32[1024,128]{1,0:T(8,128)S(1)} %fusion.33), kind=kOutput, calls=%fused_computation.17 | convolution fusion | flops 1879834624 | bytes 24379392 | tf_op jit(solution)/shard_map/dot_general | solution.py:82
  119.1 0.6 copy-done.5
  120.7 0.2 fusion.21
  120.9 2.4 scatter_custom_fusion
  123.7 5.2 gather_fusion
  128.9 7.9 %gather.9 = bf16[128,5,3584]{2,1,0:T(8,128)(2,1)} reshape(bf16[640,3584]{1,0:T(8,128)(2,1)} %gather_fusion) | data formatting | bytes 9175040 | tf_op jit(solution)/shard_map/gather | solution.py:54
  136.8 3.9 broadcast_select_fusion
  140.7 110.0 %all_to_all.16 = bf16[128,5,3584]{2,1,0:T(8,128)(2,1)} all-to-all(bf16[128,5,3584]{2,1,0:T(8,128)(2,1)S(1)} %broadcast_select_fusion), channel_id=1, replica_groups=mesh['row_0'=4,'row_1'=2,'col'=16] {'row_0','row_1','col'}, dimensions={0} | all-to-all | bytes 9175040 | tf_op jit(solution)/shard_map/all_to_all | solution.py:56
  250.7 8.3 %reshape.78 = bf16[640,3584]{1,0:T(8,128)(2,1)} reshape(bf16[128,5,3584]{2,1,0:T(8,128)(2,1)} %all_to_all.16) | data formatting | bytes 9175040 | tf_op jit(solution)/shard_map/reshape | solution.py:64
  259.1 69.9 %reduce-scatter.3.cloned.1.call-done = f32[256,3584]{1,0:T(8,128)} async-done(((f32[1024,3584]{1,0:T(8,128)}), f32[256,3584]{1,0:T(8,128)}) %reduce-scatter.3.cloned.1.call-update) | async-done | bytes 3670032 | tf_op jit(solution)/shard_map/reduce_scatter | solution.py:13
  329.0 10.9 %fusion.4 = f32[640,1024]{1,0:T(8,128)} fusion(bf16[640,3584]{1,0:T(8,128)(2,1)} %reshape.78, bf16[1,3584,1024]{2,1,0:T(8,128)(2,1)} %param.12), kind=kOutput, calls=%fused_computation.7 | convolution fusion | flops 4697620480 | bytes 14548992 | tf_op jit(solution)/shard_map/dot_general | solution.py:18
  339.9 18.8 %fusion.6 = bf16[640,3584]{1,0:T(8,128)(2,1)} fusion(bf16[1,1024,3584]{2,1,0:T(8,128)(2,1)} %param.14, f32[640,1024]{1,0:T(8,128)} %fusion.4, bf16[640,3584]{1,0:T(8,128)(2,1)} %reshape.78, bf16[1,3584,1024]{2,1,0:T(8,128)(2,1)} %param.13), kind=kOutput, calls=%fused_computation.11 | convolution fusion | flops 9401466880 | bytes 26476544 | tf_op jit(solution)/shard_map/dot_general | solution.py:21
  358.7 7.8 %reshape.79 = bf16[128,5,3584]{2,1,0:T(8,128)(2,1)} reshape(bf16[640,3584]{1,0:T(8,128)(2,1)} %fusion.6) | data formatting | bytes 9175040 | tf_op jit(solution)/shard_map/reshape | solution.py:67
  366.5 11.8 %all-to-all-start.1 = ((bf16[128,5,3584]{2,1,0:T(8,128)(2,1)}), bf16[128,5,3584]{2,1,0:T(8,128)(2,1)}, u32[]{:S(2)}, u32[]{:S(2)}) async-start(bf16[128,5,3584]{2,1,0:T(8,128)(2,1)} %reshape.79), calls=%async_computation.1 | async-start | bytes 14680064 | tf_op jit(solution)/shard_map/all_to_all | solution.py:66
  378.5 103.8 %all-to-all-done.1 = bf16[128,5,3584]{2,1,0:T(8,128)(2,1)} async-done(((bf16[128,5,3584]{2,1,0:T(8,128)(2,1)}), bf16[128,5,3584]{2,1,0:T(8,128)(2,1)}, u32[]{:S(2)}, u32[]{:S(2)}) %all-to-all-start.1) | async-done | bytes 4587552 | tf_op jit(solution)/shard_map/all_to_all | solution.py:66
  482.2 8.1 %reshape.80 = bf16[640,3584]{1,0:T(8,128)(2,1)} reshape(bf16[128,5,3584]{2,1,0:T(8,128)(2,1)} %all-to-all-done.1) | data formatting | bytes 9175040 | tf_op jit(solution)/shard_map/reshape | solution.py:73
  490.4 10.8 %gather_fusion.1 = bf16[512,3584]{1,0:T(8,128)(2,1)} fusion(bf16[640,3584]{1,0:T(8,128)(2,1)} %reshape.80, s32[1024]{0:T(1024)S(1)} %pad_clamp_fusion), kind=kCustom, calls=%fused_computation.1 | custom fusion | bytes 7342080 | tf_op jit(solution)/shard_map/gather | solution.py:74
  501.2 7.5 %reshape.82 = f32[128,4,3584]{2,1,0:T(4,128)} reshape(bf16[512,3584]{1,0:T(8,128)(2,1)} %gather_fusion.1) | data formatting | bytes 11010048 | tf_op jit(solution)/shard_map/convert_element_type | solution.py:75
  508.7 8.3 %multiply_reduce_fusion = f32[128,3584]{1,0:T(8,128)S(1)} fusion(f32[128,4,3584]{2,1,0:T(4,128)} %reshape.82, f32[128,4]{1,0:T(8,128)S(1)} %copy.16), kind=kLoop, calls=%fused_computation.9 | loop fusion | flops 3211264 | bytes 9177088 | tf_op jit(solution)/shard_map/reduce_sum | solution.py:75
  517.0 2.6 add_convert_fusion
  (42 shorter events, 1.5 us)
Async XLA Ops:
  6.5 96.5 %copy-start = (bf16[128,3584]{1,0:T(8,128)(2,1)S(1)}, bf16[128,3584]{1,0:T(8,128)(2,1)}, u32[]{:S(2)}) copy-start(bf16[128,3584]{1,0:T(8,128)(2,1)} %param.17) | copy-start | bytes 2752516
  6.5 322.4 %reduce-scatter.3.cloned.1.call-start = ((), (), s32[]{:S(2)}) async-start(), calls=%async_computation.5 | async-start | bytes 18350080 | tf_op jit(solution)/shard_map/reduce_scatter | solution.py:13
  8.4 92.6 %copy-start.7 = (bf16[3584,128]{1,0:T(8,128)(2,1)S(1)}, bf16[3584,128]{1,0:T(8,128)(2,1)}, u32[]{:S(2)}) copy-start(bf16[3584,128]{1,0:T(8,128)(2,1)} %param.15) | copy-start | bytes 2752516
  98.1 2.9 copy-start.3
  101.0 2.1 copy-start.4
  119.0 0.7 copy-start.5
  119.0 4.6 copy-start.2
  119.0 398.0 %reduce-scatter.5.cloned.1.call-start = ((), (), s32[]{:S(2)}) async-start(), calls=%async_computation.6 | async-start | bytes 5505024 | tf_op jit(solution)/shard_map/reduce_scatter | solution.py:13
  366.5 11.8 %copy-start.6 = (f32[128,4]{0,1:T(4,128)S(1)}, f32[128,4]{0,1:T(4,128)}, u32[]{:S(2)}) copy-start(f32[128,4]{0,1:T(4,128)} %param.11) | copy-start | bytes 6148
  366.5 115.7 %all-to-all-start.1 = ((bf16[128,5,3584]{2,1,0:T(8,128)(2,1)}), bf16[128,5,3584]{2,1,0:T(8,128)(2,1)}, u32[]{:S(2)}, u32[]{:S(2)}) async-start(bf16[128,5,3584]{2,1,0:T(8,128)(2,1)} %reshape.79), calls=%async_computation.1 | async-start | bytes 14680064 | tf_op jit(solution)/shard_map/all_to_all | solution.py:66
  508.7 10.9 %copy-start.1 = (bf16[128,3584]{1,0:T(8,128)(2,1)S(1)}, bf16[128,3584]{1,0:T(8,128)(2,1)}, u32[]{:S(2)}) copy-start(bf16[128,3584]{1,0:T(8,128)(2,1)} %param.17) | copy-start | bytes 2752516
Sparse Core Ops, SparseCore 0:
  119.1 209.7 reduce-scatter.2
  331.3 59.4 reduce-scatter.4
